TPU v7x, 32 devices: a whole 2x2x4 slice. The times are simulated.
32 devices in a mesh: gx: 4 (over z), gy: 2 (over y), gz: 4 (over x, core).
Axes of the slice: x: 2, y: 2, z: 4, core: 2. Of those that a mesh axis runs over, the one named last changes fastest.
Arguments:
- amplitudes: bfloat16 [1792, 16384], P(('gz', 'gy'), 'gx'), may hold values from -6 to 6
- virt_integrals: bfloat16 [16384, 16384], P('gx', ('gy', 'gz')), may hold values from -0.046875 to 0.046875
- occ_integrals: bfloat16 [1792, 1792], P('gz'), may hold values from -0.125 to 0.125
- occ_irrep: int32 [1792], P(('gz', 'gy')), may hold values from 0 to 7, as said below
- virt_irrep: int32 [16384], P('gx'), may hold values from 0 to 7, as said below
Outputs:
- ladder_term: float32 [1792, 16384], P(('gz', 'gx'), 'gy')
- hole_term: float32 [1792, 16384], P('gz', ('gx', 'gy'))
Inputs may be any that keep to these rules, and one draw needn't show every extreme that they name: `occ_irrep`: labels never fall along the array and come in runs of whole multiples of 64 pairs. `virt_irrep`: labels never fall along the array and come in runs of whole multiples of 64 pairs.
All inputs are finite; a program needn't handle non-finite values.
Results may differ from a plain program's by a relative error of at most 0.0003.
Values may be sent and summed in bfloat16 or wider, within the bound.
No kernel may reach another device: no remote copies, remote signals or barrier semaphores. Data moves between devices by JAX's collectives and lax.ppermute only.
A program may use at most 192 MiB of HBM per device.

v0:
```python
import functools

import jax
import jax.numpy as jnp
from jax import lax
from jax.experimental import pallas as pl
from jax.experimental.pallas import tpu as pltpu
from jax.sharding import PartitionSpec as P

F32 = jnp.float32
CODE = jnp.int16
TAIL = 16
FINE = 64.0
LOG_TOP = 29.9
SMALLEST = 1e-27


def coded(value):
    largest = jnp.maximum(jnp.max(jnp.abs(value)), SMALLEST)
    level = jnp.ceil(jnp.log2(jnp.full((TAIL, value.shape[1]), largest, F32)) * FINE)
    factor = jnp.exp2(LOG_TOP - level[:1] * (1.0 / FINE))
    size = jnp.abs(value) * factor
    size = (size * lax.rsqrt(jnp.maximum(size, 1e-6)) + 0.5).astype(jnp.int32)
    return jnp.where(value < 0.0, -size, size).astype(CODE), level.astype(jnp.int32).astype(CODE)


def decoded(ref, rows):
    code = ref[:rows, :].astype(jnp.int32).astype(F32)
    level = ref[rows:, :].astype(jnp.int32).astype(F32)[:1]
    return code * jnp.abs(code) * jnp.exp2(level * (1.0 / FINE) - LOG_TOP)


def write_coded(ref, value, start, width):
    rows = value.shape[0]
    code, level = coded(value)
    ref[:rows, start:start + width] = code
    ref[rows:, start:start + width] = level


def products_kernel(options, flag_ref, *refs):
    count, inputs = len(options), 2 * sum(options)
    rows_refs, integrals_ref = refs[:inputs], refs[inputs]
    out_refs, code_refs = refs[inputs + 1:inputs + count + 1], refs[inputs + count + 1:]
    rows, cols = 2 * rows_refs[0].shape[0], integrals_ref.shape[1]
    width = min(cols, 512)
    step, last = pl.program_id(0), pl.num_programs(0) - 1

    @pl.when(step == 0)
    def _():
        for out_ref in out_refs:
            out_ref[...] = jnp.zeros_like(out_ref)

    blocks, at = [], 0
    for option in options:
        pair = [rows_ref[...] for rows_ref in rows_refs[at:at + 2]]
        if option == 2:
            pair = [jnp.where(flag_ref[0] == 1, one, rows_refs[at + 2 + i][...]) for i, one in enumerate(pair)]
        blocks += pair
        at += 2 * option
    gathered = jnp.concatenate(blocks, axis=0)
    for start in range(0, cols, width):
        value = jnp.dot(gathered, integrals_ref[:, start:start + width], preferred_element_type=F32)
        for index, out_ref in enumerate(out_refs):
            out_ref[:, start:start + width] += value[rows * index:rows * (index + 1)]

    @pl.when(step == last)
    def _():
        for out_ref, code_ref in zip(out_refs, code_refs):
            for start in range(0, cols, width):
                write_coded(code_ref, out_ref[:, start:start + width], start, width)


def products(groups, integrals, flag):
    part, depth = groups[0][0][0].shape
    options, cols = [len(group) for group in groups], integrals.shape[1]
    blocks = [block for group in groups for pair in group for block in pair]
    block, count, rows = min(depth, 1024), len(groups), 2 * part
    results = pl.pallas_call(
        functools.partial(products_kernel, options),
        grid_spec=pltpu.PrefetchScalarGridSpec(
            num_scalar_prefetch=1,
            grid=(depth // block,),
            in_specs=[pl.BlockSpec((part, block), lambda k, _: (0, k))] * len(blocks)
            + [pl.BlockSpec((block, cols), lambda k, _: (k, 0))],
            out_specs=[pl.BlockSpec((rows, cols), lambda k, _: (0, 0))] * count
            + [pl.BlockSpec((rows + TAIL, cols), lambda k, _: (0, 0))] * count,
        ),
        out_shape=[jax.ShapeDtypeStruct((rows, cols), F32)] * count
        + [jax.ShapeDtypeStruct((rows + TAIL, cols), CODE)] * count,
        compiler_params=pltpu.CompilerParams(vmem_limit_bytes=40 << 20),
        cost_estimate=pl.CostEstimate(flops=2_000_000_000, bytes_accessed=2_000_000, transcendentals=0),
    )(flag.astype(jnp.int32).reshape(1), *blocks, integrals)
    return list(zip(results[:count], results[count:]))


def sums_kernel(kind, bases, choices, arrivals, flags_ref, *refs):
    base_refs, refs = refs[:bases], refs[bases:]
    choice_refs, refs = refs[:choices], refs[choices:]
    arrival_refs, out_refs, total_ref = refs[:arrivals], refs[arrivals:-1], refs[-1]
    rows, width = total_ref.shape
    for index, base_ref in enumerate(base_refs):

        @pl.when(flags_ref[0] == index)
        def _():
            total_ref[...] = base_ref[...]

    for index, choice_ref in enumerate(choice_refs):

        @pl.when(flags_ref[1] == index)
        def _():
            total_ref[...] += decoded(choice_ref, rows)

    total = total_ref[...]
    for arrival_ref in arrival_refs:
        total += decoded(arrival_ref, rows)
    each = rows // len(out_refs)
    for index, out_ref in enumerate(out_refs):
        own = total[each * index:each * (index + 1)]
        if kind == "plain":
            out_ref[...] = own
        else:
            write_coded(out_ref, own, 0, width)


def sums(kind, outs, bases, base, choices, choice, arrivals):
    rows, cols = bases[0].shape
    width = min(cols, 512)
    each = rows // outs + (0 if kind == "plain" else TAIL)
    return pl.pallas_call(
        functools.partial(sums_kernel, kind, len(bases), len(choices), len(arrivals)),
        grid_spec=pltpu.PrefetchScalarGridSpec(
            num_scalar_prefetch=1,
            grid=(cols // width,),
            in_specs=[pl.BlockSpec((rows, width), lambda j, _: (0, j))] * len(bases)
            + [pl.BlockSpec((rows + TAIL, width), lambda j, _: (0, j))] * (len(choices) + len(arrivals)),
            out_specs=[pl.BlockSpec((each, width), lambda j, _: (0, j))] * outs,
            scratch_shapes=[pltpu.VMEM((rows, width), F32)],
        ),
        out_shape=[jax.ShapeDtypeStruct((each, cols), F32 if kind == "plain" else CODE)] * outs,
        compiler_params=pltpu.CompilerParams(vmem_limit_bytes=40 << 20),
        cost_estimate=pl.CostEstimate(flops=1_000_000, bytes_accessed=1_000_000, transcendentals=0),
    )(jnp.stack([base, choice]).astype(jnp.int32), *bases, *choices, *arrivals)


def assemble_kernel(place_ref, own_ref, sibling_ref, *refs):
    coded_refs, out_ref = refs[:-1], refs[-1]
    flip = pl.program_id(0) ^ place_ref[0]

    @pl.when(flip == 0)
    def _():
        out_ref[...] = own_ref[...]

    @pl.when(flip == 1)
    def _():
        out_ref[...] = sibling_ref[...]

    for index, coded_ref in enumerate(coded_refs):

        @pl.when(flip == 2 + index)
        def _():
            out_ref[...] = decoded(coded_ref, out_ref.shape[0])


def assemble(place, own, sibling, *others):
    rows, cols = own.shape
    return pl.pallas_call(
        assemble_kernel,
        grid_spec=pltpu.PrefetchScalarGridSpec(
            num_scalar_prefetch=1,
            grid=(4,),
            in_specs=[pl.BlockSpec((rows, cols), lambda j, _: (0, 0))] * 2
            + [pl.BlockSpec((rows + TAIL, cols), lambda j, _: (0, 0))] * 2,
            out_specs=pl.BlockSpec((rows, cols), lambda j, _: (0, j)),
        ),
        out_shape=jax.ShapeDtypeStruct((rows, 4 * cols), F32),
        compiler_params=pltpu.CompilerParams(vmem_limit_bytes=40 << 20),
        cost_estimate=pl.CostEstimate(flops=1_000_000, bytes_accessed=1_000_000, transcendentals=0),
    )(place.astype(jnp.int32).reshape(1), own, sibling, *others)


def hole_kernel(count, places_ref, *refs):
    rows_refs, occ_ref = refs[:count], refs[count]
    out_ref, columns_ref = refs[-2:]
    part = rows_refs[0].shape[0]
    for index, rows_ref in enumerate(rows_refs):
        start = pl.multiple_of(places_ref[index] * part, part)
        columns_ref[pl.ds(start, part), :] = rows_ref[...]
    out_ref[...] = jnp.dot(occ_ref[...], columns_ref[...], preferred_element_type=F32)


def hole_product(occ, row_blocks, places, half):
    part, depth = row_blocks[0].shape
    cols = depth // 2
    width = min(cols, 512)
    steps = cols // width
    return pl.pallas_call(
        functools.partial(hole_kernel, len(row_blocks)),
        grid_spec=pltpu.PrefetchScalarGridSpec(
            num_scalar_prefetch=1,
            grid=(steps,),
            in_specs=[pl.BlockSpec((part, width), lambda j, scalars: (0, scalars[len(row_blocks)] * steps + j))] * len(row_blocks)
            + [pl.BlockSpec(occ.shape, lambda j, scalars: (0, 0))],
            out_specs=pl.BlockSpec((occ.shape[0], width), lambda j, scalars: (0, j)),
            scratch_shapes=[pltpu.VMEM((occ.shape[1], width), occ.dtype)],
        ),
        out_shape=jax.ShapeDtypeStruct((occ.shape[0], cols), F32),
        compiler_params=pltpu.CompilerParams(vmem_limit_bytes=32 << 20),
        cost_estimate=pl.CostEstimate(flops=2_000_000_000, bytes_accessed=2_000_000, transcendentals=0),
    )(jnp.stack([*places, half]).astype(jnp.int32), *row_blocks, occ)


def masked_rows(amplitudes, occ_irrep, virt_irrep):
    keep = occ_irrep[:, None] == virt_irrep[None, :]
    return jnp.where(keep, amplitudes, jnp.zeros_like(amplitudes))


def whole_sums(amplitudes, virt_integrals, occ_integrals, occ_irrep, virt_irrep):
    masked = masked_rows(amplitudes, occ_irrep, virt_irrep)
    rows = lax.all_gather(masked, ("gz", "gy"), axis=0, tiled=True)
    partial = jnp.dot(rows, virt_integrals, preferred_element_type=F32)
    nx, nz = lax.axis_size("gx"), lax.axis_size("gz")
    by_owner = partial.reshape(nz, nx, -1, partial.shape[1]).swapaxes(0, 1)
    mine = lax.psum_scatter(by_owner, "gx", scatter_dimension=0, tiled=True)
    ladder_term = lax.all_to_all(mine[0], "gz", split_axis=0, concat_axis=2, tiled=True)[0]
    width = rows.shape[1] // lax.axis_size("gy")
    columns = lax.dynamic_slice_in_dim(rows, lax.axis_index("gy") * width, width, 1)
    hole_term = jnp.dot(occ_integrals, columns, preferred_element_type=F32)
    return ladder_term, hole_term


def line_of_four(amplitudes, virt_integrals, occ_integrals, occ_irrep, virt_irrep):
    z, y, g = (lax.axis_index(name) for name in ("gx", "gy", "gz"))
    mirrored = z >= 2
    first = (y == 1) != mirrored
    inner = (z == 1) | (z == 2)
    part = amplitudes.shape[0] // 2

    def over_gz(value, flip):
        return lax.ppermute(value, "gz", [(i, i ^ flip) for i in range(4)])

    def sibling(value):
        return over_gz(value, 1)

    def over_gy(value):
        return lax.ppermute(value, "gy", [(0, 1), (1, 0)])

    def inward(code):
        return lax.ppermute(code, "gx", [(0, 1), (3, 2)])

    def across(code):
        return lax.ppermute(code, "gx", [(1, 2), (2, 1)])

    def inward_two(code):
        return lax.ppermute(code, "gx", [(0, 2), (3, 1)])

    def outward_two(code):
        return lax.ppermute(code, "gx", [(1, 3), (2, 0)])

    def outward(code):
        return lax.ppermute(code, "gx", [(2, 3), (1, 0)])

    def own_part(start):
        rows = lax.dynamic_slice_in_dim(amplitudes, start, part, 0)
        labels = lax.dynamic_slice_in_dim(occ_irrep, start, part, 0)
        return masked_rows(rows, labels, virt_irrep)

    def pick(condition, one, other):
        return jnp.where(condition, one, other)

    def stage(work):
        skipped = jax.tree.map(lambda leaf: jnp.zeros(leaf.shape, leaf.dtype), jax.eval_shape(work))
        return lax.cond(z < 4, work, lambda: skipped)

    def times(*groups):
        return products(groups, virt_integrals, first)

    second = ~first
    none = jnp.int32(0)

    def plus(choices, bases):
        which = second if len(bases) == 2 else none
        return sums("coded", 1, bases, which, choices, which, [])[0]

    odd = pick(mirrored, 0, part)
    high, low = own_part(odd), own_part(part - odd)

    def work0():
        x_high, y_high, s_high = over_gz(high, 2), over_gy(high), sibling(high)
        (near,) = times([(high, s_high)])
        return x_high, y_high, s_high, near

    x_high, y_high, s_high, (q_near, p0) = stage(work0)

    def work1():
        a0, yx_high, y_low = inward(p0), over_gz(y_high, 2), over_gy(low)
        sx_high, sy_high = sibling(x_high), sibling(y_high)
        (after,) = times([(x_high, sx_high), (y_high, sy_high)])
        return a0, yx_high, y_low, sx_high, sy_high, after

    a0, yx_high, y_low, sx_high, sy_high, (q_after, p1) = stage(work1)
    two = pick(first, low, y_low)

    def work2():
        a1, x_two, syx_high, s_two = inward(p1), over_gz(two, 2), sibling(yx_high), sibling(two)
        third, two_near = times([(y_high, sy_high), (yx_high, syx_high)], [(two, s_two)])
        return a1, x_two, syx_high, s_two, pick(first, y_low, low), third, two_near[1]

    a1, x_two, syx_high, s_two, zero, (q_third, p2), p5 = stage(work2)

    def work3():
        a2, m_near, x_zero, sx_two = inward(p2), across(p5), over_gz(zero, 2), sibling(x_two)
        b0 = plus([a0, a1], [q_near, q_after])
        (two_far,) = times([(x_two, sx_two)])
        return a2, m_near, x_zero, sx_two, b0, two_far

    a2, m_near, x_zero, sx_two, p_b0, (q_two_far, p3) = stage(work3)

    def work4():
        a3, b0, s_zero, sx_zero = inward(p3), outward_two(p_b0), sibling(zero), sibling(x_zero)
        b1 = plus([a1, a2], [q_after, q_third])
        (rest,) = times([(yx_high, syx_high), (x_high, sx_high)])
        return a3, b0, s_zero, sx_zero, b1, rest

    a3, b0, s_zero, sx_zero, p_b1, (q_rest, p4) = stage(work4)

    def work5():
        a4, b1 = inward(p4), outward_two(p_b1)
        b2 = plus([a3], [q_two_far])
        (zero_far,) = times([(x_zero, sx_zero)])
        return a4, b1, b2, zero_far

    a4, b1, p_b2, (q_zero_far, p6) = stage(work5)
    ends = pick(inner, 0, 1)

    def work6():
        b2, o_far = across(p_b2), outward(p6)
        (zero_near,) = times([(zero, s_zero)])
        (far,) = sums("plain", 1, [q_rest, q_zero_far], ends, [a4, b1], ends, [])
        return zero_near, sums("coded", 2, [far], none, [b2, o_far], ends, [])

    (q_zero_near, p7), (far_one, far_two) = stage(work6)

    def owner(index):
        return pick(mirrored, 3 - index, index)

    held = (
        (owner(pick(first, 3, 1)), (high, s_high, x_high, sx_high)),
        (owner(pick(first, 1, 3)), (y_high, sy_high, yx_high, syx_high)),
        (owner(2), (two, s_two, x_two, sx_two)),
        (owner(0), (zero, s_zero, x_zero, sx_zero)),
    )
    row_blocks = [block for _, group in held for block in group]
    places = [(g ^ flip) * 4 + place for place, _ in held for flip in range(4)]

    def work7():
        e_near, o_near, block_two, block_three = inward_two(p5), outward(p7), over_gz(far_one, 2), over_gz(far_two, 3)
        base = pick(inner, pick(first, 0, 1), 2)
        (almost,) = sums("plain", 1, [q_third, q_near, q_zero_near], base, [a2, a0, b0], base, [m_near])
        hole_term = hole_product(occ_integrals, row_blocks, places, y)
        return (block_two, block_three, hole_term, *sums("plain", 2, [almost], none, [e_near, o_near], ends, []))

    block_two, block_three, hole_term, near_one, near_two = stage(work7)
    ladder_term = assemble(g, near_one, sibling(near_two), block_two, block_three)
    return ladder_term, hole_term


def solution(mesh):
    placed = (P(("gz", "gy"), "gx"), P("gx", ("gy", "gz")), P("gz", None), P(("gz", "gy")), P("gx"))
    sizes = tuple(mesh.shape[name] for name in ("gx", "gy", "gz"))
    return jax.shard_map(
        line_of_four if sizes == (4, 2, 4) else whole_sums,
        mesh=mesh,
        in_specs=placed,
        out_specs=(P(("gz", "gx"), "gy"), P("gz", ("gx", "gy"))),
        check_vma=False,
    )
```

profile of v0, /device:TPU:13, one launch (start us, length us, event | category | flops | bytes accessed | tf_op | source)
XLA Modules:
  0.0 229.9 jit_solution(4120914514483533910)
XLA Ops:
  4.4 23.7 %conditional.8 = (bf16[112,4096]{1,0:T(8,128)(2,1)}, bf16[112,4096]{1,0:T(8,128)(2,1)}, bf16[112,4096]{1,0:T(8,128)(2,1)}, f32[224,2048]{1,0:T(8,128)}, s16[240,2048]{1,0:T(8,128)(2,1)}) conditional(s32[]{:T(128)} %convert_element_type.9, () %tuple.94, (bf16[112,4096]{1,0:T(8,128)(2,1)S(1)}, pred[]{:T(512)}, bf16[4096,2048]{1,0:T(8,128)(2,1)}) %tuple.95), branch_computations={%region_0.1_spmd, %region_1.2_spmd} | conditional | flops 2000000000 | bytes 13010213 | solution.py:272
  7.3 11.5 %branch_1_fun.15 = (f32[224,2048]{1,0:T(8,128)}, s16[240,2048]{1,0:T(8,128)(2,1)}) custom-call(s32[1]{0:T(128)} %bitcast.flag_ref, bf16[112,4096]{1,0:T(8,128)(2,1)S(1)} %get-tuple-element.276.refs_0_, bf16[112,4096]{1,0:T(8,128)(2,1)} %collective-permute-done.2.refs_1_, bf16[4096,2048]{1,0:T(8,128)(2,1)} %get-tuple-element.278.refs_2_), custom_call_target="tpu_custom_call" | custom-call | flops 2000000000 | bytes 2000000 | tf_op jit(solution)/shard_map/cond/branch_1_fun/pallas_call | solution.py:78
  18.8 8.3 %collective-permute-done = bf16[112,4096]{1,0:T(8,128)(2,1)} collective-permute-done((bf16[112,4096]{1,0:T(8,128)(2,1)S(1)}, bf16[112,4096]{1,0:T(8,128)(2,1)}, u32[]{:S(2)}, u32[]{:S(2)}) %collective-permute-start) | collective-permute-done | bytes 917536 | tf_op jit(solution)/shard_map/cond/branch_1_fun/ppermute | solution.py:239
  28.0 26.1 %conditional.9 = (s16[240,2048]{1,0:T(8,128)(2,1)}, bf16[112,4096]{1,0:T(8,128)(2,1)}, bf16[112,4096]{1,0:T(8,128)(2,1)}, bf16[112,4096]{1,0:T(8,128)(2,1)}, bf1...) conditional(s32[]{:T(128)} %convert_element_type.9, () %tuple.93, ...), branch_computations={%region_2.3_spmd, %region_3.4_spmd} | conditional | flops 2000000000 | bytes 20612484 | solution.py:272
  32.9 12.2 %branch_1_fun.16 = (f32[224,2048]{1,0:T(8,128)}, s16[240,2048]{1,0:T(8,128)(2,1)}) custom-call(s32[1]{0:T(128)} %bitcast.1.flag_ref, bf16[112,4096]{1,0:T(8,128)(2,1)} %get-tuple-element.284.refs_0_, bf16[112,4096]{1,0:T(8,128)(2,1)} %collective-permute-done.6.refs_1_, bf16[112,4096]{1,0:T(8,128)(2,1)} %get-tuple-element.282.refs_2_, ...), custom_call_target="tpu_custom_call" | custom-call | flops 2000000000 | bytes 2000000 | tf_op jit(solution)/shard_map/cond/branch_1_fun/pallas_call | solution.py:78
  45.1 7.2 %collective-permute-done.4 = bf16[112,4096]{1,0:T(8,128)(2,1)} collective-permute-done((bf16[112,4096]{1,0:T(8,128)(2,1)}, bf16[112,4096]{1,0:T(8,128)(2,1)}, u32[]{:S(2)}, u32[]{:S(2)}) %collective-permute-start.4) | collective-permute-done | bytes 917536 | tf_op jit(solution)/shard_map/cond/branch_1_fun/ppermute | solution.py:239
  55.2 27.3 %conditional.10 = (s16[240,2048]{1,0:T(8,128)(2,1)}, bf16[112,4096]{1,0:T(8,128)(2,1)}, bf16[112,4096]{1,0:T(8,128)(2,1)}, bf16[112,4096]{1,0:T(8,128)(2,1)}, bf...) conditional(s32[]{:T(128)} %convert_element_type.9, () %tuple.92, ...), branch_computations={%region_4.5_spmd, %region_5.6_spmd} | conditional | flops 2000458752 | bytes 19694948 | solution.py:272
  60.6 16.5 %branch_1_fun.17 = (f32[224,2048]{1,0:T(8,128)S(1)}, f32[224,2048]{1,0:T(8,128)}, s16[240,2048]{1,0:T(8,128)(2,1)}, s16[240,2048]{1,0:T(8,128)(2,1)}) custom-call(s32[1]{0:T(128)} %bitcast.2.flag_ref, bf16[112,4096]{1,0:T(8,128)(2,1)} %get-tuple-element.295.refs_0_, bf16[112,4096]{1,0:T(8,128)(2,1)} %get-tuple-element.296.refs_1_, ...), custom_call_target="tpu_custom_call" | custom-call | flops 2000000000 | bytes 2000000 | tf_op jit(solution)/shard_map/cond/branch_1_fun/pallas_call | solution.py:78
  82.5 29.1 %conditional.11 = (s16[240,2048]{1,0:T(8,128)(2,1)}, s16[240,2048]{1,0:T(8,128)(2,1)}, bf16[112,4096]{1,0:T(8,128)(2,1)}, bf16[112,4096]{1,0:T(8,128)(2,1)}, s16...) conditional(s32[]{:T(128)} %convert_element_type.9, () %tuple.99, ...), branch_computations={%region_6.7_spmd, %region_7.8_spmd} | conditional | flops 2001000064 | bytes 18204582 | solution.py:272
  90.7 5.3 %branch_1_fun.18 = s16[240,2048]{1,0:T(8,128)(2,1)S(1)} custom-call(s32[2]{0:T(128)S(1)} %add_convert_fusion.flags_ref, f32[224,2048]{1,0:T(8,128)} %get-tuple-element.306.refs_0_, f32[224,2048]{1,0:T(8,128)} %get-tuple-element.307.refs_1_, s16[240,2048]{1,0:T(8,128)(2,1)} %get-tuple-element.308.refs_2_, s16[240,2048]{1,0:T(8,128)(2,1)} %get-tuple-element.309.refs_3_), custom_call_target="tpu_custom_call" | custom-call | flops 1000000 | bytes 1000000 | tf_op jit(solution)/shard_map/cond/branch_1_fun/pallas_call | solution.py:129
  96.0 11.8 %branch_1_fun.19 = (f32[224,2048]{1,0:T(8,128)}, s16[240,2048]{1,0:T(8,128)(2,1)}) custom-call(s32[1]{0:T(128)} %bitcast.4.flag_ref, bf16[112,4096]{1,0:T(8,128)(2,1)} %get-tuple-element.304.refs_0_, bf16[112,4096]{1,0:T(8,128)(2,1)} %collective-permute-done.17.refs_1_, bf16[4096,2048]{1,0:T(8,128)(2,1)} %get-tuple-element.311.refs_2_), custom_call_target="tpu_custom_call" | custom-call | flops 2000000000 | bytes 2000000 | tf_op jit(solution)/shard_map/cond/branch_1_fun/pallas_call | solution.py:78
  111.6 27.6 %conditional.12 = (s16[240,2048]{1,0:T(8,128)(2,1)}, s16[240,2048]{1,0:T(8,128)(2,1)}, bf16[112,4096]{1,0:T(8,128)(2,1)}, bf16[112,4096]{1,0:T(8,128)(2,1)}, s16...) conditional(s32[]{:T(128)} %convert_element_type.9, () %tuple.98, ...), branch_computations={%region_8.9_spmd, %region_9.10_spmd} | conditional | flops 2001000064 | bytes 18204582 | solution.py:272
  112.9 6.9 %collective-permute-start.19 = (s16[240,2048]{1,0:T(8,128)(2,1)S(1)}, s16[240,2048]{1,0:T(8,128)(2,1)}, u32[]{:S(2)}, u32[]{:S(2)}) collective-permute-start(s16[240,2048]{1,0:T(8,128)(2,1)S(1)} %get-tuple-element.315), channel_id=1, source_target_pairs={{8,24},{16,0},{9,25},{17,1},{10,26},{18,2},{11,27},{19,3},{12,28},... | collective-permute-start | bytes 2949128 | tf_op jit(solution)/shard_map/cond/branch_1_fun/ppermute | solution.py:257
  121.3 5.8 %branch_1_fun.20 = s16[240,2048]{1,0:T(8,128)(2,1)} custom-call(s32[2]{0:T(128)S(1)} %add_convert_fusion.1.flags_ref, f32[224,2048]{1,0:T(8,128)} %get-tuple-element.319.refs_0_, f32[224,2048]{1,0:T(8,128)S(1)} %get-tuple-element.320.refs_1_, s16[240,2048]{1,0:T(8,128)(2,1)} %get-tuple-element.321.refs_2_, s16[240,2048]{1,0:T(8,128)(2,1)} %get-tuple-element.322.refs_3_), custom_call_target="tpu_custom_call" | custom-call | flops 1000000 | bytes 1000000 | tf_op jit(solution)/shard_map/cond/branch_1_fun/pallas_call | solution.py:129
  127.1 12.1 %branch_1_fun.21 = (f32[224,2048]{1,0:T(8,128)}, s16[240,2048]{1,0:T(8,128)(2,1)}) custom-call(s32[1]{0:T(128)} %bitcast.6.flag_ref, bf16[112,4096]{1,0:T(8,128)(2,1)} %get-tuple-element.324.refs_0_, bf16[112,4096]{1,0:T(8,128)(2,1)} %get-tuple-element.325.refs_1_, bf16[112,4096]{1,0:T(8,128)(2,1)} %get-tuple-element.326.refs_2_, ...), custom_call_target="tpu_custom_call" | custom-call | flops 2000000000 | bytes 2000000 | tf_op jit(solution)/shard_map/cond/branch_1_fun/pallas_call | solution.py:78
  139.2 26.3 %conditional.13 = (s16[240,2048]{1,0:T(8,128)(2,1)}, s16[240,2048]{1,0:T(8,128)(2,1)}, s16[240,2048]{1,0:T(8,128)(2,1)}, f32[224,2048]{1,0:T(8,128)}, s16[240,2048]{1,0:T(8,128)(2,1)}) conditional(s32[]{:T(128)} %convert_element_type.9, () %tuple.102, (s16[240,2048]{1,0:T(8,128)(2,1)}, s16[240,2048]{1,0:T(8,128)(2,1)}, f32[224,2048]{1,0:T(8,128)}, ...), branch_computations={%region_10.11_spmd, %region_11.12_spmd} | conditional | flops 2001000064 | bytes 10864457 | solution.py:272
  140.5 6.6 %collective-permute-start.9 = (s16[240,2048]{1,0:T(8,128)(2,1)}, s16[240,2048]{1,0:T(8,128)(2,1)}, u32[]{:S(2)}, u32[]{:S(2)}) collective-permute-start(s16[240,2048]{1,0:T(8,128)(2,1)} %get-tuple-element.332), channel_id=1, source_target_pairs={{8,24},{16,0},{9,25},{17,1},{10,26},{18,2},{11,27},{19,3},{12,28},... | collective-permute-start | bytes 2949128 | tf_op jit(solution)/shard_map/cond/branch_1_fun/ppermute | solution.py:257
  147.2 5.5 %branch_1_fun.22 = s16[240,2048]{1,0:T(8,128)(2,1)} custom-call(s32[2]{0:T(128)S(1)} %broadcast_36_flags_ref.0.flags_ref, f32[224,2048]{1,0:T(8,128)} %get-tuple-element.333.refs_0_, s16[240,2048]{1,0:T(8,128)(2,1)} %get-tuple-element.334.refs_1_), custom_call_target="tpu_custom_call" | custom-call | flops 1000000 | bytes 1000000 | tf_op jit(solution)/shard_map/cond/branch_1_fun/pallas_call | solution.py:129
  152.7 11.7 %branch_1_fun.23 = (f32[224,2048]{1,0:T(8,128)}, s16[240,2048]{1,0:T(8,128)(2,1)}) custom-call(s32[1]{0:T(128)} %bitcast.7.flag_ref, bf16[112,4096]{1,0:T(8,128)(2,1)} %get-tuple-element.336.refs_0_, bf16[112,4096]{1,0:T(8,128)(2,1)} %get-tuple-element.337.refs_1_, bf16[4096,2048]{1,0:T(8,128)(2,1)} %get-tuple-element.338.refs_2_), custom_call_target="tpu_custom_call" | custom-call | flops 2000000000 | bytes 2000000 | tf_op jit(solution)/shard_map/cond/branch_1_fun/pallas_call | solution.py:78
  165.6 26.8 %conditional.14 = (f32[224,2048]{1,0:T(8,128)}, s16[240,2048]{1,0:T(8,128)(2,1)}, s16[128,2048]{1,0:T(8,128)(2,1)S(1)}, s16[128,2048]{1,0:T(8,128)(2,1)S(1)}) conditional(s32[]{:T(128)} %convert_element_type.9, () %tuple.91, (pred[]{:T(512)}, bf16[112,4096]{1,0:T(8,128)(2,1)}, bf16[112,4096]{1,0:T(8,128)(2,1)}, bf16[4096,2048]{1,0:T(8,128)(2,1)}, ...), branch_computations={%region_12.13_spmd, %region_13.14_spmd} | conditional | flops 2001999872 | bytes 11864461 | solution.py:272
  175.2 11.8 %branch_1_fun.24 = (f32[224,2048]{1,0:T(8,128)}, s16[240,2048]{1,0:T(8,128)(2,1)}) custom-call(s32[1]{0:T(128)} %bitcast.8.flag_ref, bf16[112,4096]{1,0:T(8,128)(2,1)} %get-tuple-element.342.refs_0_, bf16[112,4096]{1,0:T(8,128)(2,1)} %get-tuple-element.343.refs_1_, bf16[4096,2048]{1,0:T(8,128)(2,1)} %get-tuple-element.344.refs_2_), custom_call_target="tpu_custom_call" | custom-call | flops 2000000000 | bytes 2000000 | tf_op jit(solution)/shard_map/cond/branch_1_fun/pallas_call | solution.py:78
  192.4 30.9 %conditional.15 = (s16[128,2048]{1,0:T(8,128)(2,1)}, s16[128,2048]{1,0:T(8,128)(2,1)}, f32[448,2048]{1,0:T(8,128)}, f32[112,2048]{1,0:T(8,128)}, f32[112,2048]{1,0:T(8,128)}) conditional(s32[]{:T(128)} %convert_element_type.9, () %tuple.90, (s16[128,2048]{1,0:T(8,128)(2,1)S(1)}, s16[128,2048]{1,0:T(8,128)(2,1)S(1)}, s32[]{:T(128)}, pred[]{:T(512)}, ...), branch_computations={%region_14.15_spmd, %region_15.16_spmd} | conditional | flops 2001999872 | bytes 29822036 | solution.py:272
  204.5 5.5 %branch_1_fun.28.refs_0_ = f32[224,2048]{1,0:T(8,128)S(1)} custom-call(s32[2]{0:T(128)S(1)} %pad_add_fusion.3.flags_ref, f32[224,2048]{1,0:T(8,128)} %get-tuple-element.381.refs_0_, f32[224,2048]{1,0:T(8,128)} %get-tuple-element.382.refs_1_, f32[224,2048]{1,0:T(8,128)} %get-tuple-element.383.refs_2_, s16[240,2048]{1,0:T(8,128)(2,1)} %get-tuple-element.384.refs_3_, ...), custom_call_target="tpu_custom_call" | custom-call | flops 1000000 | bytes 1000000 | tf_op jit(solution)/shard_map/cond/branch_1_fun/pallas_call | solution.py:129
  210.2 8.5 %branch_1_fun.27 = f32[448,2048]{1,0:T(8,128)} custom-call(s32[17]{0:T(128)S(1)} %stack.87.places_ref, bf16[112,4096]{1,0:T(8,128)(2,1)S(1)} %copy-done.4, bf16[112,4096]{1,0:T(8,128)(2,1)} %get-tuple-element.363.refs_1_, bf16[112,4096]{1,0:T(8,128)(2,1)} %get-tuple-element.364.refs_2_, bf16[112,4096]{1,0:T(8,128)(2,1)} %get-tuple-element.365.refs_3_, ...), custom_call_target="tpu_custom_call" | custom-call | flops 2000000000 | bytes 2000000 | tf_op jit(solution)/shard_map/cond/branch_1_fun/pallas_call | solution.py:196
  (81 shorter events, 81.7 us)
Async XLA Ops:
  5.1 22.1 %collective-permute-start = (bf16[112,4096]{1,0:T(8,128)(2,1)S(1)}, bf16[112,4096]{1,0:T(8,128)(2,1)}, u32[]{:S(2)}, u32[]{:S(2)}) collective-permute-start(bf16[112,4096]{1,0:T(8,128)(2,1)S(1)} %get-tuple-element.276.refs_0_), channel_id=1, source_target_pairs={{0,2},{1,3},{2,0},{3,1},{4,6},{5,7},{6,4},{7,5},{8,10},{9,11},{10,... | collective-permute-start | bytes 2752520 | tf_op jit(solution)/shard_map/cond/branch_1_fun/ppermute | solution.py:239
  6.3 21.8 %collective-permute-start.1 = (bf16[112,4096]{1,0:T(8,128)(2,1)S(1)}, bf16[112,4096]{1,0:T(8,128)(2,1)}, u32[]{:S(2)}, u32[]{:S(2)}) collective-permute-start(bf16[112,4096]{1,0:T(8,128)(2,1)S(1)} %get-tuple-element.276.refs_0_), channel_id=1, source_target_pairs={{0,4},{4,0},{1,5},{5,1},{2,6},{6,2},{3,7},{7,3},{8,12},{12,8},{9,1... | collective-permute-start | bytes 2752520 | tf_op jit(solution)/shard_map/cond/branch_1_fun/ppermute | solution.py:245
  29.2 25.0 %collective-permute-start.3 = (s16[240,2048]{1,0:T(8,128)(2,1)}, s16[240,2048]{1,0:T(8,128)(2,1)}, u32[]{:S(2)}, u32[]{:S(2)}) collective-permute-start(s16[240,2048]{1,0:T(8,128)(2,1)} %get-tuple-element.281), channel_id=1, source_target_pairs={{0,8},{24,16},{1,9},{25,17},{2,10},{26,18},{3,11},{27,19},{4,12},{... | collective-permute-start | bytes 2949128 | tf_op jit(solution)/shard_map/cond/branch_1_fun/ppermute | solution.py:248
  30.4 21.8 %collective-permute-start.4 = (bf16[112,4096]{1,0:T(8,128)(2,1)}, bf16[112,4096]{1,0:T(8,128)(2,1)}, u32[]{:S(2)}, u32[]{:S(2)}) collective-permute-start(bf16[112,4096]{1,0:T(8,128)(2,1)} %get-tuple-element.282.refs_2_), channel_id=1, source_target_pairs={{0,2},{1,3},{2,0},{3,1},{4,6},{5,7},{6,4},{7,5},{8,10},{9,11},{10,... | collective-permute-start | bytes 2752520 | tf_op jit(solution)/shard_map/cond/branch_1_fun/ppermute | solution.py:239
  30.8 21.5 %collective-permute-start.5 = (bf16[112,4096]{1,0:T(8,128)(2,1)S(1)}, bf16[112,4096]{1,0:T(8,128)(2,1)}, u32[]{:S(2)}, u32[]{:S(2)}) collective-permute-start(bf16[112,4096]{1,0:T(8,128)(2,1)S(1)} %get-tuple-element.283), channel_id=1, source_target_pairs={{0,4},{4,0},{1,5},{5,1},{2,6},{6,2},{3,7},{7,3},{8,12},{12,8},{9,1... | collective-permute-start | bytes 2752520 | tf_op jit(solution)/shard_map/cond/branch_1_fun/ppermute | solution.py:245
  55.2 5.4 %collective-permute-start.13 = (bf16[112,4096]{1,0:T(8,128)(2,1)S(1)}, bf16[112,4096]{1,0:T(8,128)(2,1)}, u32[]{:S(2)}, u32[]{:S(2)}) collective-permute-start(bf16[112,4096]{1,0:T(8,128)(2,1)S(1)} %get-tuple-element.290.refs_4_), channel_id=1, source_target_pairs={{0,1},{1,0},{2,3},{3,2},{4,5},{5,4},{6,7},{7,6},{8,9},{9,8},{10,11... | collective-permute-start | bytes 2752520 | tf_op jit(solution)/shard_map/cond/branch_1_fun/ppermute | solution.py:239
  56.6 22.1 %collective-permute-start.11 = (bf16[112,4096]{1,0:T(8,128)(2,1)S(1)}, bf16[112,4096]{1,0:T(8,128)(2,1)}, u32[]{:S(2)}, u32[]{:S(2)}) collective-permute-start(bf16[112,4096]{1,0:T(8,128)(2,1)S(1)} %get-tuple-element.290.refs_4_), channel_id=1, source_target_pairs={{0,2},{1,3},{2,0},{3,1},{4,6},{5,7},{6,4},{7,5},{8,10},{9,11},{10,... | collective-permute-start | bytes 2752520 | tf_op jit(solution)/shard_map/cond/branch_1_fun/ppermute | solution.py:239
  57.1 25.4 %collective-permute-start.10 = (s16[240,2048]{1,0:T(8,128)(2,1)}, s16[240,2048]{1,0:T(8,128)(2,1)}, u32[]{:S(2)}, u32[]{:S(2)}) collective-permute-start(s16[240,2048]{1,0:T(8,128)(2,1)} %get-tuple-element.289), channel_id=1, source_target_pairs={{0,8},{24,16},{1,9},{25,17},{2,10},{26,18},{3,11},{27,19},{4,12},{... | collective-permute-start | bytes 2949128 | tf_op jit(solution)/shard_map/cond/branch_1_fun/ppermute | solution.py:248
  82.5 13.5 %collective-permute-start.17 = (bf16[112,4096]{1,0:T(8,128)(2,1)}, bf16[112,4096]{1,0:T(8,128)(2,1)}, u32[]{:S(2)}, u32[]{:S(2)}) collective-permute-start(bf16[112,4096]{1,0:T(8,128)(2,1)} %get-tuple-element.304.refs_0_), channel_id=1, source_target_pairs={{0,1},{1,0},{2,3},{3,2},{4,5},{5,4},{6,7},{7,6},{8,9},{9,8},{10,11... | collective-permute-start | bytes 2752520 | tf_op jit(solution)/shard_map/cond/branch_1_fun/ppermute | solution.py:239
  83.5 27.9 %collective-permute-start.14 = (s16[240,2048]{1,0:T(8,128)(2,1)}, s16[240,2048]{1,0:T(8,128)(2,1)}, u32[]{:S(2)}, u32[]{:S(2)}) collective-permute-start(s16[240,2048]{1,0:T(8,128)(2,1)} %get-tuple-element.301), channel_id=1, source_target_pairs={{0,8},{24,16},{1,9},{25,17},{2,10},{26,18},{3,11},{27,19},{4,12},{... | collective-permute-start | bytes 2949128 | tf_op jit(solution)/shard_map/cond/branch_1_fun/ppermute | solution.py:248
  84.8 26.8 %collective-permute-start.15 = (s16[240,2048]{1,0:T(8,128)(2,1)}, s16[240,2048]{1,0:T(8,128)(2,1)}, u32[]{:S(2)}, u32[]{:S(2)}) collective-permute-start(s16[240,2048]{1,0:T(8,128)(2,1)} %get-tuple-element.302), channel_id=1, source_target_pairs={{8,16},{16,8},{9,17},{17,9},{10,18},{18,10},{11,19},{19,11},{12,20... | collective-permute-start | bytes 2949128 | tf_op jit(solution)/shard_map/cond/branch_1_fun/ppermute | solution.py:251
  89.4 22.0 %collective-permute-start.16 = (bf16[112,4096]{1,0:T(8,128)(2,1)}, bf16[112,4096]{1,0:T(8,128)(2,1)}, u32[]{:S(2)}, u32[]{:S(2)}) collective-permute-start(bf16[112,4096]{1,0:T(8,128)(2,1)} %get-tuple-element.303), channel_id=1, source_target_pairs={{0,2},{1,3},{2,0},{3,1},{4,6},{5,7},{6,4},{7,5},{8,10},{9,11},{10,... | collective-permute-start | bytes 2752520 | tf_op jit(solution)/shard_map/cond/branch_1_fun/ppermute | solution.py:239
  111.6 27.6 %collective-permute-start.18 = (s16[240,2048]{1,0:T(8,128)(2,1)}, s16[240,2048]{1,0:T(8,128)(2,1)}, u32[]{:S(2)}, u32[]{:S(2)}) collective-permute-start(s16[240,2048]{1,0:T(8,128)(2,1)} %get-tuple-element.314), channel_id=1, source_target_pairs={{0,8},{24,16},{1,9},{25,17},{2,10},{26,18},{3,11},{27,19},{4,12},{... | collective-permute-start | bytes 2949128 | tf_op jit(solution)/shard_map/cond/branch_1_fun/ppermute | solution.py:248
  112.9 26.3 %collective-permute-start.19 = (s16[240,2048]{1,0:T(8,128)(2,1)S(1)}, s16[240,2048]{1,0:T(8,128)(2,1)}, u32[]{:S(2)}, u32[]{:S(2)}) collective-permute-start(s16[240,2048]{1,0:T(8,128)(2,1)S(1)} %get-tuple-element.315), channel_id=1, source_target_pairs={{8,24},{16,0},{9,25},{17,1},{10,26},{18,2},{11,27},{19,3},{12,28},... | collective-permute-start | bytes 2949128 | tf_op jit(solution)/shard_map/cond/branch_1_fun/ppermute | solution.py:257
  119.8 19.4 %collective-permute-start.20 = (bf16[112,4096]{1,0:T(8,128)(2,1)}, bf16[112,4096]{1,0:T(8,128)(2,1)}, u32[]{:S(2)}, u32[]{:S(2)}) collective-permute-start(bf16[112,4096]{1,0:T(8,128)(2,1)} %get-tuple-element.316), channel_id=1, source_target_pairs={{0,1},{1,0},{2,3},{3,2},{4,5},{5,4},{6,7},{7,6},{8,9},{9,8},{10,11... | collective-permute-start | bytes 2752520 | tf_op jit(solution)/shard_map/cond/branch_1_fun/ppermute | solution.py:239
  121.2 18.0 %collective-permute-start.21 = (bf16[112,4096]{1,0:T(8,128)(2,1)}, bf16[112,4096]{1,0:T(8,128)(2,1)}, u32[]{:S(2)}, u32[]{:S(2)}) collective-permute-start(bf16[112,4096]{1,0:T(8,128)(2,1)} %get-tuple-element.317), channel_id=1, source_target_pairs={{0,1},{1,0},{2,3},{3,2},{4,5},{5,4},{6,7},{7,6},{8,9},{9,8},{10,11... | collective-permute-start | bytes 2752520 | tf_op jit(solution)/shard_map/cond/branch_1_fun/ppermute | solution.py:239
  139.2 25.1 %collective-permute-start.8 = (s16[240,2048]{1,0:T(8,128)(2,1)}, s16[240,2048]{1,0:T(8,128)(2,1)}, u32[]{:S(2)}, u32[]{:S(2)}) collective-permute-start(s16[240,2048]{1,0:T(8,128)(2,1)} %get-tuple-element.331), channel_id=1, source_target_pairs={{0,8},{24,16},{1,9},{25,17},{2,10},{26,18},{3,11},{27,19},{4,12},{... | collective-permute-start | bytes 2949128 | tf_op jit(solution)/shard_map/cond/branch_1_fun/ppermute | solution.py:248
  140.5 25.0 %collective-permute-start.9 = (s16[240,2048]{1,0:T(8,128)(2,1)}, s16[240,2048]{1,0:T(8,128)(2,1)}, u32[]{:S(2)}, u32[]{:S(2)}) collective-permute-start(s16[240,2048]{1,0:T(8,128)(2,1)} %get-tuple-element.332), channel_id=1, source_target_pairs={{8,24},{16,0},{9,25},{17,1},{10,26},{18,2},{11,27},{19,3},{12,28},... | collective-permute-start | bytes 2949128 | tf_op jit(solution)/shard_map/cond/branch_1_fun/ppermute | solution.py:257
  165.6 22.4 %collective-permute-start.22 = (s16[240,2048]{1,0:T(8,128)(2,1)}, s16[240,2048]{1,0:T(8,128)(2,1)S(1)}, u32[]{:S(2)}, u32[]{:S(2)}) collective-permute-start(s16[240,2048]{1,0:T(8,128)(2,1)} %get-tuple-element.352), channel_id=1, source_target_pairs={{8,16},{16,8},{9,17},{17,9},{10,18},{18,10},{11,19},{19,11},{12,20... | collective-permute-start | bytes 2949128 | tf_op jit(solution)/shard_map/cond/branch_1_fun/ppermute | solution.py:251
  168.1 21.2 %collective-permute-start.23 = (s16[240,2048]{1,0:T(8,128)(2,1)}, s16[240,2048]{1,0:T(8,128)(2,1)S(1)}, u32[]{:S(2)}, u32[]{:S(2)}) collective-permute-start(s16[240,2048]{1,0:T(8,128)(2,1)} %get-tuple-element.353), channel_id=1, source_target_pairs={{16,24},{8,0},{17,25},{9,1},{18,26},{10,2},{19,27},{11,3},{20,28},... | collective-permute-start | bytes 2949128 | tf_op jit(solution)/shard_map/cond/branch_1_fun/ppermute | solution.py:260
  192.4 26.2 %collective-permute-start.26 = (s16[240,2048]{1,0:T(8,128)(2,1)}, s16[240,2048]{1,0:T(8,128)(2,1)S(1)}, u32[]{:S(2)}, u32[]{:S(2)}) collective-permute-start(s16[240,2048]{1,0:T(8,128)(2,1)} %get-tuple-element.388), channel_id=1, source_target_pairs={{0,16},{24,8},{1,17},{25,9},{2,18},{26,10},{3,19},{27,11},{4,20},{... | collective-permute-start | bytes 2949128 | tf_op jit(solution)/shard_map/cond/branch_1_fun/ppermute | solution.py:254
  193.7 25.0 %collective-permute-start.27 = (s16[240,2048]{1,0:T(8,128)(2,1)}, s16[240,2048]{1,0:T(8,128)(2,1)S(1)}, u32[]{:S(2)}, u32[]{:S(2)}) collective-permute-start(s16[240,2048]{1,0:T(8,128)(2,1)} %get-tuple-element.389), channel_id=1, source_target_pairs={{16,24},{8,0},{17,25},{9,1},{18,26},{10,2},{19,27},{11,3},{20,28},... | collective-permute-start | bytes 2949128 | tf_op jit(solution)/shard_map/cond/branch_1_fun/ppermute | solution.py:260
  198.3 23.3 %collective-permute-start.24 = (s16[128,2048]{1,0:T(8,128)(2,1)S(1)}, s16[128,2048]{1,0:T(8,128)(2,1)}, u32[]{:S(2)}, u32[]{:S(2)}) collective-permute-start(s16[128,2048]{1,0:T(8,128)(2,1)S(1)} %get-tuple-element.356), channel_id=1, source_target_pairs={{0,2},{1,3},{2,0},{3,1},{4,6},{5,7},{6,4},{7,5},{8,10},{9,11},{10,... | collective-permute-start | bytes 1572872 | tf_op jit(solution)/shard_map/cond/branch_1_fun/ppermute | solution.py:239
  199.5 23.8 %collective-permute-start.25 = (s16[128,2048]{1,0:T(8,128)(2,1)S(1)}, s16[128,2048]{1,0:T(8,128)(2,1)}, u32[]{:S(2)}, u32[]{:S(2)}) collective-permute-start(s16[128,2048]{1,0:T(8,128)(2,1)S(1)} %get-tuple-element.357), channel_id=1, source_target_pairs={{0,3},{1,2},{2,1},{3,0},{4,7},{5,6},{6,5},{7,4},{8,11},{9,10},{10,... | collective-permute-start | bytes 1572872 | tf_op jit(solution)/shard_map/cond/branch_1_fun/ppermute | solution.py:239
  (11 other events, 64.6 us)
where the time goes:
time: 233 us; the launch traced here: 230 us
  Pallas kernels  132 us (57%)
  starting transfers between devices  51.3 us (22%)
  waiting for transfers between devices  38.1 us (16%)
  other arithmetic  4.66 us (2%)
  local copies, waits for them, and re-layouts  2.78 us (1%)
    pallas_call x7, Pallas kernels, products(): pl.pallas_call(functools.partial(products_kernel, options), grid_spec=plt...  87.5 us
    pallas_call x7, Pallas kernels, sums(): pl.pallas_call(functools.partial(sums_kernel, kind, len(bases), len(choic...  32.4 us
    ppermute x15, waiting for transfers between devices, over_gz(): return lax.ppermute(value, 'gz', [(i, i ^ flip) for i in range(4)])  27.7 us
    ppermute x15, starting transfers between devices, over_gz(): return lax.ppermute(value, 'gz', [(i, i ^ flip) for i in range(4)])  15 us
    ppermute x2, starting transfers between devices, outward_two(): return lax.ppermute(code, 'gx', [(1, 3), (2, 0)])  13.6 us
    pallas_call x1, Pallas kernels, hole_product(): pl.pallas_call(functools.partial(hole_kernel, len(row_blocks)), grid_spec...  8.47 us
    ppermute x2, starting transfers between devices, outward(): return lax.ppermute(code, 'gx', [(2, 3), (1, 0)])  7.48 us
    ppermute x2, starting transfers between devices, across(): return lax.ppermute(code, 'gx', [(1, 2), (2, 1)])  7.06 us
  transfers between devices with their start and end apart: 29, of which 16 were waited for; matrix products, arithmetic and copies ran while one was open for 1% of the time, Pallas kernels for 54%

commit v1 on v0

--- a/solution.py
+++ b/solution.py
@@ -87,8 +87,8 @@
         ),
         out_shape=[jax.ShapeDtypeStruct((rows, cols), F32)] * count
         + [jax.ShapeDtypeStruct((rows + TAIL, cols), CODE)] * count,
-        compiler_params=pltpu.CompilerParams(vmem_limit_bytes=40 << 20),
-        cost_estimate=pl.CostEstimate(flops=2_000_000_000, bytes_accessed=2_000_000, transcendentals=0),
+        compiler_params=pltpu.CompilerParams(vmem_limit_bytes=52 << 20),
+        cost_estimate=pl.CostEstimate(flops=1_000_000, bytes_accessed=1_000_000, transcendentals=0),
     )(flag.astype(jnp.int32).reshape(1), *blocks, integrals)
     return list(zip(results[:count], results[count:]))
 
@@ -137,7 +137,7 @@
             scratch_shapes=[pltpu.VMEM((rows, width), F32)],
         ),
         out_shape=[jax.ShapeDtypeStruct((each, cols), F32 if kind == "plain" else CODE)] * outs,
-        compiler_params=pltpu.CompilerParams(vmem_limit_bytes=40 << 20),
+        compiler_params=pltpu.CompilerParams(vmem_limit_bytes=52 << 20),
         cost_estimate=pl.CostEstimate(flops=1_000_000, bytes_accessed=1_000_000, transcendentals=0),
     )(jnp.stack([base, choice]).astype(jnp.int32), *bases, *choices, *arrivals)
 
@@ -173,7 +173,7 @@
             out_specs=pl.BlockSpec((rows, cols), lambda j, _: (0, j)),
         ),
         out_shape=jax.ShapeDtypeStruct((rows, 4 * cols), F32),
-        compiler_params=pltpu.CompilerParams(vmem_limit_bytes=40 << 20),
+        compiler_params=pltpu.CompilerParams(vmem_limit_bytes=52 << 20),
         cost_estimate=pl.CostEstimate(flops=1_000_000, bytes_accessed=1_000_000, transcendentals=0),
     )(place.astype(jnp.int32).reshape(1), own, sibling, *others)
 
@@ -204,8 +204,8 @@
             scratch_shapes=[pltpu.VMEM((occ.shape[1], width), occ.dtype)],
         ),
         out_shape=jax.ShapeDtypeStruct((occ.shape[0], cols), F32),
-        compiler_params=pltpu.CompilerParams(vmem_limit_bytes=32 << 20),
-        cost_estimate=pl.CostEstimate(flops=2_000_000_000, bytes_accessed=2_000_000, transcendentals=0),
+        compiler_params=pltpu.CompilerParams(vmem_limit_bytes=52 << 20),
+        cost_estimate=pl.CostEstimate(flops=1_000_000, bytes_accessed=1_000_000, transcendentals=0),
     )(jnp.stack([*places, half]).astype(jnp.int32), *row_blocks, occ)
 
 
@@ -294,51 +294,36 @@
     def work1():
         a0, yx_high, y_low = inward(p0), over_gz(y_high, 2), over_gy(low)
         sx_high, sy_high = sibling(x_high), sibling(y_high)
-        (after,) = times([(x_high, sx_high), (y_high, sy_high)])
-        return a0, yx_high, y_low, sx_high, sy_high, after
-
-    a0, yx_high, y_low, sx_high, sy_high, (q_after, p1) = stage(work1)
-    two = pick(first, low, y_low)
+        ((q_after, p1),) = times([(x_high, sx_high), (y_high, sy_high)])
+        a1, syx_high = inward(p1), sibling(yx_high)
+        two, zero = pick(first, low, y_low), pick(first, y_low, low)
+        x_two, s_two = over_gz(two, 2), sibling(two)
+        third, (_, p5) = times([(y_high, sy_high), (yx_high, syx_high)], [(two, s_two)])
+        return a0, a1, yx_high, sx_high, sy_high, syx_high, two, zero, x_two, s_two, q_after, third, p5
+
+    a0, a1, yx_high, sx_high, sy_high, syx_high, two, zero, x_two, s_two, q_after, (q_third, p2), p5 = stage(work1)
 
     def work2():
-        a1, x_two, syx_high, s_two = inward(p1), over_gz(two, 2), sibling(yx_high), sibling(two)
-        third, two_near = times([(y_high, sy_high), (yx_high, syx_high)], [(two, s_two)])
-        return a1, x_two, syx_high, s_two, pick(first, y_low, low), third, two_near[1]
-
-    a1, x_two, syx_high, s_two, zero, (q_third, p2), p5 = stage(work2)
+        a2, m_near, x_zero, sx_two, s_zero = inward(p2), across(p5), over_gz(zero, 2), sibling(x_two), sibling(zero)
+        ((q_two_far, p3),) = times([(x_two, sx_two)])
+        a3, b0 = inward(p3), outward_two(plus([a0, a1], [q_near, q_after]))
+        (rest,) = times([(yx_high, syx_high), (x_high, sx_high)])
+        b1 = plus([a1, a2], [q_after, q_third])
+        return a2, m_near, x_zero, sx_two, s_zero, a3, b0, rest, b1, q_two_far
+
+    a2, m_near, x_zero, sx_two, s_zero, a3, b0, (q_rest, p4), p_b1, q_two_far = stage(work2)
+    ends = pick(inner, 0, 1)
 
     def work3():
-        a2, m_near, x_zero, sx_two = inward(p2), across(p5), over_gz(zero, 2), sibling(x_two)
-        b0 = plus([a0, a1], [q_near, q_after])
-        (two_far,) = times([(x_two, sx_two)])
-        return a2, m_near, x_zero, sx_two, b0, two_far
-
-    a2, m_near, x_zero, sx_two, p_b0, (q_two_far, p3) = stage(work3)
-
-    def work4():
-        a3, b0, s_zero, sx_zero = inward(p3), outward_two(p_b0), sibling(zero), sibling(x_zero)
-        b1 = plus([a1, a2], [q_after, q_third])
-        (rest,) = times([(yx_high, syx_high), (x_high, sx_high)])
-        return a3, b0, s_zero, sx_zero, b1, rest
-
-    a3, b0, s_zero, sx_zero, p_b1, (q_rest, p4) = stage(work4)
-
-    def work5():
-        a4, b1 = inward(p4), outward_two(p_b1)
-        b2 = plus([a3], [q_two_far])
-        (zero_far,) = times([(x_zero, sx_zero)])
-        return a4, b1, b2, zero_far
-
-    a4, b1, p_b2, (q_zero_far, p6) = stage(work5)
-    ends = pick(inner, 0, 1)
-
-    def work6():
-        b2, o_far = across(p_b2), outward(p6)
+        a4, b1, sx_zero = inward(p4), outward_two(p_b1), sibling(x_zero)
+        b2 = across(plus([a3], [q_two_far]))
+        ((q_zero_far, p6),) = times([(x_zero, sx_zero)])
+        o_far = outward(p6)
         (zero_near,) = times([(zero, s_zero)])
         (far,) = sums("plain", 1, [q_rest, q_zero_far], ends, [a4, b1], ends, [])
-        return zero_near, sums("coded", 2, [far], none, [b2, o_far], ends, [])
-
-    (q_zero_near, p7), (far_one, far_two) = stage(work6)
+        return sx_zero, zero_near, sums("coded", 2, [far], none, [b2, o_far], ends, [])
+
+    sx_zero, (q_zero_near, p7), (far_one, far_two) = stage(work3)
 
     def owner(index):
         return pick(mirrored, 3 - index, index)
@@ -352,14 +337,14 @@
     row_blocks = [block for _, group in held for block in group]
     places = [(g ^ flip) * 4 + place for place, _ in held for flip in range(4)]
 
-    def work7():
+    def work4():
         e_near, o_near, block_two, block_three = inward_two(p5), outward(p7), over_gz(far_one, 2), over_gz(far_two, 3)
         base = pick(inner, pick(first, 0, 1), 2)
         (almost,) = sums("plain", 1, [q_third, q_near, q_zero_near], base, [a2, a0, b0], base, [m_near])
         hole_term = hole_product(occ_integrals, row_blocks, places, y)
         return (block_two, block_three, hole_term, *sums("plain", 2, [almost], none, [e_near, o_near], ends, []))
 
-    block_two, block_three, hole_term, near_one, near_two = stage(work7)
+    block_two, block_three, hole_term, near_one, near_two = stage(work4)
     ladder_term = assemble(g, near_one, sibling(near_two), block_two, block_three)
     return ladder_term, hole_term
 

time: 233 us -> 238 us (1.021)
  starting transfers between devices: 51.3 us -> 45.8 us
  other arithmetic: 4.66 us -> 8.09 us
  waiting for transfers between devices: 38.1 us -> 40.7 us
    ppermute x2, waiting for transfers between devices: 1.21 us -> 11.1 us  [across(): return lax.ppermute(code, 'gx', [(1, 2), (2, 1)])]
    ppermute x15, waiting for transfers between devices: 27.7 us -> 18.6 us  [over_gz(): return lax.ppermute(value, 'gz', [(i, i ^ flip) for i in range(4)])]
    ppermute x2, waiting for transfers between devices: 0.9 us -> 8.81 us  [over_gy(): return lax.ppermute(value, 'gy', [(0, 1), (1, 0)])]
    ppermute x5, waiting for transfers between devices: 5.76 us -> 0.01 us  [inward(): return lax.ppermute(code, 'gx', [(0, 1), (3, 2)])]
    pallas_call x7, Pallas kernels: 32.4 us -> 35.9 us  [sums(): pl.pallas_call(functools.partial(sums_kernel, kind, len(bases), len(choic...]
    select_n x1 -> x2, other arithmetic: 1.97 us -> 4.85 us  [masked_rows(): return jnp.where(keep, amplitudes, jnp.zeros_like(amplitudes))]
    ppermute x2, starting transfers between devices: 7.06 us -> 4.22 us  [across(): return lax.ppermute(code, 'gx', [(1, 2), (2, 1)])]
  transfers between devices with their start and end apart: 29 -> 29, of which waited for: 16 -> 14; matrix products, arithmetic and copies ran while one was open for 1% -> 3% of each run, Pallas kernels for 54% -> 54%
where the time goes in v1:
time: 238 us; the launch traced here: 234 us
  Pallas kernels  134 us (56%)
  starting transfers between devices  45.8 us (19%)
  waiting for transfers between devices  40.7 us (17%)
  other arithmetic  8.09 us (3%)
  local copies, waits for them, and re-layouts  4.31 us (2%)
    pallas_call x7, Pallas kernels, products(): pl.pallas_call(functools.partial(products_kernel, options), grid_spec=plt...  85.8 us
    pallas_call x7, Pallas kernels, sums(): pl.pallas_call(functools.partial(sums_kernel, kind, len(bases), len(choic...  35.9 us
    ppermute x15, waiting for transfers between devices, over_gz(): return lax.ppermute(value, 'gz', [(i, i ^ flip) for i in range(4)])  18.6 us
    ppermute x15, starting transfers between devices, over_gz(): return lax.ppermute(value, 'gz', [(i, i ^ flip) for i in range(4)])  13.8 us
    ppermute x2, starting transfers between devices, outward_two(): return lax.ppermute(code, 'gx', [(1, 3), (2, 0)])  12.7 us
    ppermute x2, waiting for transfers between devices, across(): return lax.ppermute(code, 'gx', [(1, 2), (2, 1)])  11.1 us
    ppermute x2, waiting for transfers between devices, over_gy(): return lax.ppermute(value, 'gy', [(0, 1), (1, 0)])  8.81 us
    pallas_call x1, Pallas kernels, hole_product(): pl.pallas_call(functools.partial(hole_kernel, len(row_blocks)), grid_spec...  8.47 us
  transfers between devices with their start and end apart: 29, of which 14 were waited for; matrix products, arithmetic and copies ran while one was open for 3% of the time, Pallas kernels for 54%

profile of v1, /device:TPU:13, one launch (start us, length us, event | category | flops | bytes accessed | tf_op | source)
XLA Modules:
  0.0 233.8 jit_solution(772599463594967304)
XLA Ops:
  3.8 23.7 %conditional.5 = (bf16[112,4096]{1,0:T(8,128)(2,1)}, bf16[112,4096]{1,0:T(8,128)(2,1)}, bf16[112,4096]{1,0:T(8,128)(2,1)}, f32[224,2048]{1,0:T(8,128)}, s16[240,2048]{1,0:T(8,128)(2,1)}) conditional(s32[]{:T(128)} %convert_element_type.5, () %tuple.71, (bf16[112,4096]{1,0:T(8,128)(2,1)S(1)}, pred[]{:T(512)}, bf16[4096,2048]{1,0:T(8,128)(2,1)}) %tuple.72), branch_computations={%region_0.1_spmd, %region_1.2_spmd} | conditional | flops 1000001 | bytes 12010213 | solution.py:272
  6.7 11.5 %branch_1_fun.15 = (f32[224,2048]{1,0:T(8,128)}, s16[240,2048]{1,0:T(8,128)(2,1)}) custom-call(s32[1]{0:T(128)} %bitcast.flag_ref, bf16[112,4096]{1,0:T(8,128)(2,1)S(1)} %get-tuple-element.246.refs_0_, bf16[112,4096]{1,0:T(8,128)(2,1)} %collective-permute-done.2.refs_1_, bf16[4096,2048]{1,0:T(8,128)(2,1)} %get-tuple-element.248.refs_2_), custom_call_target="tpu_custom_call" | custom-call | flops 1000000 | bytes 1000000 | tf_op jit(solution)/shard_map/cond/branch_1_fun/pallas_call | solution.py:78
  18.2 8.4 %collective-permute-done = bf16[112,4096]{1,0:T(8,128)(2,1)} collective-permute-done((bf16[112,4096]{1,0:T(8,128)(2,1)S(1)}, bf16[112,4096]{1,0:T(8,128)(2,1)}, u32[]{:S(2)}, u32[]{:S(2)}) %collective-permute-start) | collective-permute-done | bytes 917536 | tf_op jit(solution)/shard_map/cond/branch_1_fun/ppermute | solution.py:239
  29.9 52.4 %conditional.6 = (s16[240,2048]{1,0:T(8,128)(2,1)}, s16[240,2048]{1,0:T(8,128)(2,1)}, bf16[112,4096]{1,0:T(8,128)(2,1)}, bf16[112,4096]{1,0:T(8,128)(2,1)}, bf16...) conditional(s32[]{:T(128)} %convert_element_type.5, () %tuple.70, ...), branch_computations={%region_2.3_spmd, %region_3.4_spmd} | conditional | flops 3835013 | bytes 47483884 | solution.py:272
  36.3 10.7 %branch_1_fun.16 = (f32[224,2048]{1,0:T(8,128)S(1)}, s16[240,2048]{1,0:T(8,128)(2,1)S(1)}) custom-call(s32[1]{0:T(128)} %bitcast.1.flag_ref, bf16[112,4096]{1,0:T(8,128)(2,1)} %get-tuple-element.253.refs_0_, bf16[112,4096]{1,0:T(8,128)(2,1)S(1)} %collective-permute-done.4.refs_1_, bf16[112,4096]{1,0:T(8,128)(2,1)} %get-tuple-element.254.refs_2_.refs_0_, ...), custom_call_target="tpu_custom_call" | custom-call | flops 1000000 | bytes 1000000 | tf_op jit(solution)/shard_map/cond/branch_1_fun/pallas_call | solution.py:78
  48.3 7.9 %collective-permute-done.9 = bf16[112,4096]{1,0:T(8,128)(2,1)} collective-permute-done((bf16[112,4096]{1,0:T(8,128)(2,1)}, bf16[112,4096]{1,0:T(8,128)(2,1)}, u32[]{:S(2)}, u32[]{:S(2)}) %collective-permute-start.9) | collective-permute-done | bytes 917536 | tf_op jit(solution)/shard_map/cond/branch_1_fun/ppermute | solution.py:245
  64.2 17.2 %branch_1_fun.17 = (f32[224,2048]{1,0:T(8,128)}, f32[224,2048]{1,0:T(8,128)}, s16[240,2048]{1,0:T(8,128)(2,1)}, s16[240,2048]{1,0:T(8,128)(2,1)}) custom-call(s32[1]{0:T(128)} %bitcast.1.flag_ref, bf16[112,4096]{1,0:T(8,128)(2,1)} %get-tuple-element.254.refs_2_.refs_0_, bf16[112,4096]{1,0:T(8,128)(2,1)} %collective-permute-done.5.refs_3_.refs_1_, ...), custom_call_target="tpu_custom_call" | custom-call | flops 1000000 | bytes 1000000 | tf_op jit(solution)/shard_map/cond/branch_1_fun/pallas_call | solution.py:78
  82.3 56.6 %conditional.7 = (s16[240,2048]{1,0:T(8,128)(2,1)}, s16[240,2048]{1,0:T(8,128)(2,1)}, bf16[112,4096]{1,0:T(8,128)(2,1)}, bf16[112,4096]{1,0:T(8,128)(2,1)}, bf16...) conditional(s32[]{:T(128)} %convert_element_type.5, () %tuple.69, ...), branch_computations={%region_4.5_spmd, %region_5.6_spmd} | conditional | flops 4000006 | bytes 34409116 | solution.py:272
  85.1 5.1 %branch_1_fun.19 = s16[240,2048]{1,0:T(8,128)(2,1)S(1)} custom-call(s32[2]{0:T(128)S(1)} %add_convert_fusion.flags_ref, f32[224,2048]{1,0:T(8,128)} %get-tuple-element.273.refs_0_, f32[224,2048]{1,0:T(8,128)S(1)} %get-tuple-element.274.refs_1_.refs_0_, s16[240,2048]{1,0:T(8,128)(2,1)} %get-tuple-element.275.refs_2_, ...), custom_call_target="tpu_custom_call" | custom-call | flops 1000000 | bytes 1000000 | tf_op jit(solution)/shard_map/cond/branch_1_fun/pallas_call | solution.py:129
  90.2 6.7 %collective-permute-start.18 = (s16[240,2048]{1,0:T(8,128)(2,1)S(1)}, s16[240,2048]{1,0:T(8,128)(2,1)}, u32[]{:S(2)}, u32[]{:S(2)}) collective-permute-start(s16[240,2048]{1,0:T(8,128)(2,1)S(1)} %branch_1_fun.19), channel_id=1, source_target_pairs={{8,24},{16,0},{9,25},{17,1},{10,26},{18,2},{11,27},{19,3},{12,28},... | collective-permute-start | bytes 2949128 | tf_op jit(solution)/shard_map/cond/branch_1_fun/ppermute | solution.py:257
  99.1 11.4 %branch_1_fun.18 = (f32[224,2048]{1,0:T(8,128)}, s16[240,2048]{1,0:T(8,128)(2,1)S(1)}) custom-call(s32[1]{0:T(128)} %bitcast.2.flag_ref, bf16[112,4096]{1,0:T(8,128)(2,1)} %get-tuple-element.269.refs_0_, bf16[112,4096]{1,0:T(8,128)(2,1)} %collective-permute-done.15.refs_1_, bf16[4096,2048]{1,0:T(8,128)(2,1)} %get-tuple-element.271.refs_2_.refs_4_), custom_call_target="tpu_custom_call" | custom-call | flops 1000000 | bytes 1000000 | tf_op jit(solution)/shard_map/cond/branch_1_fun/pallas_call | solution.py:78
  113.2 11.9 %branch_1_fun.20 = (f32[224,2048]{1,0:T(8,128)}, s16[240,2048]{1,0:T(8,128)(2,1)}) custom-call(s32[1]{0:T(128)} %bitcast.2.flag_ref, bf16[112,4096]{1,0:T(8,128)(2,1)} %get-tuple-element.277.refs_0_, bf16[112,4096]{1,0:T(8,128)(2,1)} %get-tuple-element.278.refs_1_, bf16[112,4096]{1,0:T(8,128)(2,1)} %get-tuple-element.279.refs_2_, ...), custom_call_target="tpu_custom_call" | custom-call | flops 1000000 | bytes 1000000 | tf_op jit(solution)/shard_map/cond/branch_1_fun/pallas_call | solution.py:78
  125.2 5.9 %branch_1_fun.21 = s16[240,2048]{1,0:T(8,128)(2,1)} custom-call(s32[2]{0:T(128)S(1)} %add_convert_fusion.flags_ref, f32[224,2048]{1,0:T(8,128)S(1)} %get-tuple-element.274.refs_1_.refs_0_, f32[224,2048]{1,0:T(8,128)} %get-tuple-element.283.refs_1_, s16[240,2048]{1,0:T(8,128)(2,1)} %get-tuple-element.276.refs_3_.refs_2_, ...), custom_call_target="tpu_custom_call" | custom-call | flops 1000000 | bytes 1000000 | tf_op jit(solution)/shard_map/cond/branch_1_fun/pallas_call | solution.py:129
  133.2 5.8 %collective-permute-done.13 = s16[240,2048]{1,0:T(8,128)(2,1)} collective-permute-done((s16[240,2048]{1,0:T(8,128)(2,1)}, s16[240,2048]{1,0:T(8,128)(2,1)}, u32[]{:S(2)}, u32[]{:S(2)}) %collective-permute-start.13) | collective-permute-done | bytes 983072 | tf_op jit(solution)/shard_map/cond/branch_1_fun/ppermute | solution.py:251
  138.9 55.6 %conditional.8 = (bf16[112,4096]{1,0:T(8,128)(2,1)}, f32[224,2048]{1,0:T(8,128)}, s16[240,2048]{1,0:T(8,128)(2,1)}, s16[128,2048]{1,0:T(8,128)(2,1)S(1)}, s16[128,2048]{1,0:T(8,128)(2,1)}) conditional(s32[]{:T(128)} %convert_element_type.5, () %tuple.68, (bf16[112,4096]{1,0:T(8,128)(2,1)}, pred[]{:T(512)}, bf16[112,4096]{1,0:T(8,128)(2,1)}, ...), branch_computations={%region_6.7_spmd, %region_7.8_spmd} | conditional | flops 5000005 | bytes 24398940 | solution.py:272
  141.3 6.0 %collective-permute-start.21 = (s16[240,2048]{1,0:T(8,128)(2,1)}, s16[240,2048]{1,0:T(8,128)(2,1)}, u32[]{:S(2)}, u32[]{:S(2)}) collective-permute-start(s16[240,2048]{1,0:T(8,128)(2,1)} %get-tuple-element.296), channel_id=1, source_target_pairs={{8,24},{16,0},{9,25},{17,1},{10,26},{18,2},{11,27},{19,3},{12,28},... | collective-permute-start | bytes 2949128 | tf_op jit(solution)/shard_map/cond/branch_1_fun/ppermute | solution.py:257
  154.3 11.4 %branch_1_fun.23 = (f32[224,2048]{1,0:T(8,128)}, s16[240,2048]{1,0:T(8,128)(2,1)S(1)}) custom-call(s32[1]{0:T(128)} %bitcast.4.flag_ref, bf16[112,4096]{1,0:T(8,128)(2,1)} %get-tuple-element.285.refs_0_, bf16[112,4096]{1,0:T(8,128)(2,1)} %collective-permute-done.19.refs_1_, bf16[4096,2048]{1,0:T(8,128)(2,1)} %get-tuple-element.289.refs_2_), custom_call_target="tpu_custom_call" | custom-call | flops 1000000 | bytes 1000000 | tf_op jit(solution)/shard_map/cond/branch_1_fun/pallas_call | solution.py:78
  167.2 11.7 %branch_1_fun.22 = (f32[224,2048]{1,0:T(8,128)}, s16[240,2048]{1,0:T(8,128)(2,1)}) custom-call(s32[1]{0:T(128)} %bitcast.4.flag_ref, bf16[112,4096]{1,0:T(8,128)(2,1)} %get-tuple-element.287.refs_0_, bf16[112,4096]{1,0:T(8,128)(2,1)} %get-tuple-element.288.refs_1_, bf16[4096,2048]{1,0:T(8,128)(2,1)} %get-tuple-element.289.refs_2_), custom_call_target="tpu_custom_call" | custom-call | flops 1000000 | bytes 1000000 | tf_op jit(solution)/shard_map/cond/branch_1_fun/pallas_call | solution.py:78
  184.1 5.3 %collective-permute-done.22.refs_1_ = s16[240,2048]{1,0:T(8,128)(2,1)S(1)} collective-permute-done((s16[240,2048]{1,0:T(8,128)(2,1)S(1)}, s16[240,2048]{1,0:T(8,128)(2,1)S(1)}, u32[]{:S(2)}, u32[]{:S(2)}) %collective-permute-start.22) | collective-permute-done | bytes 983072 | tf_op jit(solution)/shard_map/cond/branch_1_fun/ppermute | solution.py:251
  189.4 5.1 %branch_1_fun.26 = (s16[128,2048]{1,0:T(8,128)(2,1)S(1)}, s16[128,2048]{1,0:T(8,128)(2,1)}) custom-call(s32[2]{0:T(128)S(1)} %pad_add_fusion.flags_ref, f32[224,2048]{1,0:T(8,128)} %branch_1_fun.24.refs_0_, s16[240,2048]{1,0:T(8,128)(2,1)S(1)} %collective-permute-done.22.refs_1_, s16[240,2048]{1,0:T(8,128)(2,1)S(1)} %collective-permute-done.23.refs_2_), custom_call_target="tpu_custom_call" | custom-call | flops 1000000 | bytes 1000000 | tf_op jit(solution)/shard_map/cond/branch_1_fun/pallas_call | solution.py:129
  194.5 31.4 %conditional.9 = (s16[128,2048]{1,0:T(8,128)(2,1)}, s16[128,2048]{1,0:T(8,128)(2,1)}, f32[448,2048]{1,0:T(8,128)}, f32[112,2048]{1,0:T(8,128)}, f32[112,2048]{1,0:T(8,128)}) conditional(s32[]{:T(128)} %convert_element_type.5, () %tuple.67, (s16[128,2048]{1,0:T(8,128)(2,1)S(1)}, s16[128,2048]{1,0:T(8,128)(2,1)}, s32[]{:T(128)}, pred[]{:T(512)}, ...), branch_computations={%region_8.9_spmd, %region_9.10_spmd} | conditional | flops 3000037 | bytes 36162096 | solution.py:272
  195.8 5.1 %collective-permute-start.27 = (s16[240,2048]{1,0:T(8,128)(2,1)}, s16[240,2048]{1,0:T(8,128)(2,1)S(1)}, u32[]{:S(2)}, u32[]{:S(2)}) collective-permute-start(s16[240,2048]{1,0:T(8,128)(2,1)} %get-tuple-element.335), channel_id=1, source_target_pairs={{16,24},{8,0},{17,25},{9,1},{18,26},{10,2},{19,27},{11,3},{20,28},... | collective-permute-start | bytes 2949128 | tf_op jit(solution)/shard_map/cond/branch_1_fun/ppermute | solution.py:260
  204.4 5.5 %branch_1_fun.28.refs_0_ = f32[224,2048]{1,0:T(8,128)S(1)} custom-call(s32[2]{0:T(128)S(1)} %pad_add_fusion.3.flags_ref, f32[224,2048]{1,0:T(8,128)} %get-tuple-element.327.refs_0_, f32[224,2048]{1,0:T(8,128)} %get-tuple-element.328.refs_1_, f32[224,2048]{1,0:T(8,128)} %get-tuple-element.329.refs_2_, s16[240,2048]{1,0:T(8,128)(2,1)} %get-tuple-element.330.refs_3_, ...), custom_call_target="tpu_custom_call" | custom-call | flops 1000000 | bytes 1000000 | tf_op jit(solution)/shard_map/cond/branch_1_fun/pallas_call | solution.py:129
  210.0 8.5 %branch_1_fun.27 = f32[448,2048]{1,0:T(8,128)} custom-call(s32[17]{0:T(128)S(1)} %stack.83.places_ref, bf16[112,4096]{1,0:T(8,128)(2,1)S(1)} %copy-done.5, bf16[112,4096]{1,0:T(8,128)(2,1)} %get-tuple-element.309.refs_1_, bf16[112,4096]{1,0:T(8,128)(2,1)} %get-tuple-element.310.refs_2_, bf16[112,4096]{1,0:T(8,128)(2,1)S(1)} %copy-done.3, ...), custom_call_target="tpu_custom_call" | custom-call | flops 1000000 | bytes 1000000 | tf_op jit(solution)/shard_map/cond/branch_1_fun/pallas_call | solution.py:196
  (87 shorter events, 71.8 us)
Async XLA Ops:
  4.5 22.1 %collective-permute-start = (bf16[112,4096]{1,0:T(8,128)(2,1)S(1)}, bf16[112,4096]{1,0:T(8,128)(2,1)}, u32[]{:S(2)}, u32[]{:S(2)}) collective-permute-start(bf16[112,4096]{1,0:T(8,128)(2,1)S(1)} %get-tuple-element.246.refs_0_), channel_id=1, source_target_pairs={{0,2},{1,3},{2,0},{3,1},{4,6},{5,7},{6,4},{7,5},{8,10},{9,11},{10,... | collective-permute-start | bytes 2752520 | tf_op jit(solution)/shard_map/cond/branch_1_fun/ppermute | solution.py:239
  5.7 21.8 %collective-permute-start.1 = (bf16[112,4096]{1,0:T(8,128)(2,1)S(1)}, bf16[112,4096]{1,0:T(8,128)(2,1)}, u32[]{:S(2)}, u32[]{:S(2)}) collective-permute-start(bf16[112,4096]{1,0:T(8,128)(2,1)S(1)} %get-tuple-element.246.refs_0_), channel_id=1, source_target_pairs={{0,4},{4,0},{1,5},{5,1},{2,6},{6,2},{3,7},{7,3},{8,12},{12,8},{9,1... | collective-permute-start | bytes 2752520 | tf_op jit(solution)/shard_map/cond/branch_1_fun/ppermute | solution.py:245
  29.9 6.3 %collective-permute-start.5 = (bf16[112,4096]{1,0:T(8,128)(2,1)}, bf16[112,4096]{1,0:T(8,128)(2,1)}, u32[]{:S(2)}, u32[]{:S(2)}) collective-permute-start(bf16[112,4096]{1,0:T(8,128)(2,1)} %get-tuple-element.254.refs_2_.refs_0_), channel_id=1, source_target_pairs={{0,1},{1,0},{2,3},{3,2},{4,5},{5,4},{6,7},{7,6},{8,9},{9,8},{10,11... | collective-permute-start | bytes 2752520 | tf_op jit(solution)/shard_map/cond/branch_1_fun/ppermute | solution.py:239
  34.5 21.7 %collective-permute-start.9 = (bf16[112,4096]{1,0:T(8,128)(2,1)}, bf16[112,4096]{1,0:T(8,128)(2,1)}, u32[]{:S(2)}, u32[]{:S(2)}) collective-permute-start(bf16[112,4096]{1,0:T(8,128)(2,1)} %compare_select_fusion), channel_id=1, source_target_pairs={{0,4},{4,0},{1,5},{5,1},{2,6},{6,2},{3,7},{7,3},{8,12},{12,8},{9,1... | collective-permute-start | bytes 2752520 | tf_op jit(solution)/shard_map/cond/branch_1_fun/ppermute | solution.py:245
  34.7 25.7 %collective-permute-start.7 = (bf16[112,4096]{1,0:T(8,128)(2,1)}, bf16[112,4096]{1,0:T(8,128)(2,1)}, u32[]{:S(2)}, u32[]{:S(2)}) collective-permute-start(bf16[112,4096]{1,0:T(8,128)(2,1)} %get-tuple-element.254.refs_2_.refs_0_), channel_id=1, source_target_pairs={{0,2},{1,3},{2,0},{3,1},{4,6},{5,7},{6,4},{7,5},{8,10},{9,11},{10,... | collective-permute-start | bytes 2752520 | tf_op jit(solution)/shard_map/cond/branch_1_fun/ppermute | solution.py:239
  35.0 46.5 %collective-permute-start.3 = (s16[240,2048]{1,0:T(8,128)(2,1)}, s16[240,2048]{1,0:T(8,128)(2,1)}, u32[]{:S(2)}, u32[]{:S(2)}) collective-permute-start(s16[240,2048]{1,0:T(8,128)(2,1)} %get-tuple-element.251), channel_id=1, source_target_pairs={{0,8},{24,16},{1,9},{25,17},{2,10},{26,18},{3,11},{27,19},{4,12},{... | collective-permute-start | bytes 2949128 | tf_op jit(solution)/shard_map/cond/branch_1_fun/ppermute | solution.py:248
  47.0 35.3 %collective-permute-start.6 = (s16[240,2048]{1,0:T(8,128)(2,1)S(1)}, s16[240,2048]{1,0:T(8,128)(2,1)}, u32[]{:S(2)}, u32[]{:S(2)}) collective-permute-start(s16[240,2048]{1,0:T(8,128)(2,1)S(1)} %get-tuple-element.256), channel_id=1, source_target_pairs={{0,8},{24,16},{1,9},{25,17},{2,10},{26,18},{3,11},{27,19},{4,12},{... | collective-permute-start | bytes 2949128 | tf_op jit(solution)/shard_map/cond/branch_1_fun/ppermute | solution.py:248
  60.5 21.8 %collective-permute-start.10 = (bf16[112,4096]{1,0:T(8,128)(2,1)}, bf16[112,4096]{1,0:T(8,128)(2,1)}, u32[]{:S(2)}, u32[]{:S(2)}) collective-permute-start(bf16[112,4096]{1,0:T(8,128)(2,1)} %get-tuple-element.454.refs_4_), channel_id=1, source_target_pairs={{0,2},{1,3},{2,0},{3,1},{4,6},{5,7},{6,4},{7,5},{8,10},{9,11},{10,... | collective-permute-start | bytes 2752520 | tf_op jit(solution)/shard_map/cond/branch_1_fun/ppermute | solution.py:239
  82.3 16.8 %collective-permute-start.15 = (bf16[112,4096]{1,0:T(8,128)(2,1)}, bf16[112,4096]{1,0:T(8,128)(2,1)}, u32[]{:S(2)}, u32[]{:S(2)}) collective-permute-start(bf16[112,4096]{1,0:T(8,128)(2,1)} %get-tuple-element.269.refs_0_), channel_id=1, source_target_pairs={{0,1},{1,0},{2,3},{3,2},{4,5},{5,4},{6,7},{7,6},{8,9},{9,8},{10,11... | collective-permute-start | bytes 2752520 | tf_op jit(solution)/shard_map/cond/branch_1_fun/ppermute | solution.py:239
  83.6 28.5 %collective-permute-start.12 = (s16[240,2048]{1,0:T(8,128)(2,1)}, s16[240,2048]{1,0:T(8,128)(2,1)}, u32[]{:S(2)}, u32[]{:S(2)}) collective-permute-start(s16[240,2048]{1,0:T(8,128)(2,1)} %get-tuple-element.266), channel_id=1, source_target_pairs={{0,8},{24,16},{1,9},{25,17},{2,10},{26,18},{3,11},{27,19},{4,12},{... | collective-permute-start | bytes 2949128 | tf_op jit(solution)/shard_map/cond/branch_1_fun/ppermute | solution.py:248
  90.2 43.0 %collective-permute-start.18 = (s16[240,2048]{1,0:T(8,128)(2,1)S(1)}, s16[240,2048]{1,0:T(8,128)(2,1)}, u32[]{:S(2)}, u32[]{:S(2)}) collective-permute-start(s16[240,2048]{1,0:T(8,128)(2,1)S(1)} %branch_1_fun.19), channel_id=1, source_target_pairs={{8,24},{16,0},{9,25},{17,1},{10,26},{18,2},{11,27},{19,3},{12,28},... | collective-permute-start | bytes 2949128 | tf_op jit(solution)/shard_map/cond/branch_1_fun/ppermute | solution.py:257
  96.9 42.0 %collective-permute-start.13 = (s16[240,2048]{1,0:T(8,128)(2,1)}, s16[240,2048]{1,0:T(8,128)(2,1)}, u32[]{:S(2)}, u32[]{:S(2)}) collective-permute-start(s16[240,2048]{1,0:T(8,128)(2,1)} %get-tuple-element.267), channel_id=1, source_target_pairs={{8,16},{16,8},{9,17},{17,9},{10,18},{18,10},{11,19},{19,11},{12,20... | collective-permute-start | bytes 2949128 | tf_op jit(solution)/shard_map/cond/branch_1_fun/ppermute | solution.py:251
  110.5 28.5 %collective-permute-start.17 = (s16[240,2048]{1,0:T(8,128)(2,1)S(1)}, s16[240,2048]{1,0:T(8,128)(2,1)}, u32[]{:S(2)}, u32[]{:S(2)}) collective-permute-start(s16[240,2048]{1,0:T(8,128)(2,1)S(1)} %get-tuple-element.272), channel_id=1, source_target_pairs={{0,8},{24,16},{1,9},{25,17},{2,10},{26,18},{3,11},{27,19},{4,12},{... | collective-permute-start | bytes 2949128 | tf_op jit(solution)/shard_map/cond/branch_1_fun/ppermute | solution.py:248
  111.8 21.4 %collective-permute-start.14 = (bf16[112,4096]{1,0:T(8,128)(2,1)}, bf16[112,4096]{1,0:T(8,128)(2,1)}, u32[]{:S(2)}, u32[]{:S(2)}) collective-permute-start(bf16[112,4096]{1,0:T(8,128)(2,1)} %get-tuple-element.268), channel_id=1, source_target_pairs={{0,2},{1,3},{2,0},{3,1},{4,6},{5,7},{6,4},{7,5},{8,10},{9,11},{10,... | collective-permute-start | bytes 2752520 | tf_op jit(solution)/shard_map/cond/branch_1_fun/ppermute | solution.py:239
  112.1 21.1 %collective-permute-start.16 = (bf16[112,4096]{1,0:T(8,128)(2,1)}, bf16[112,4096]{1,0:T(8,128)(2,1)}, u32[]{:S(2)}, u32[]{:S(2)}) collective-permute-start(bf16[112,4096]{1,0:T(8,128)(2,1)} %get-tuple-element.268), channel_id=1, source_target_pairs={{0,1},{1,0},{2,3},{3,2},{4,5},{5,4},{6,7},{7,6},{8,9},{9,8},{10,11... | collective-permute-start | bytes 2752520 | tf_op jit(solution)/shard_map/cond/branch_1_fun/ppermute | solution.py:239
  138.9 15.3 %collective-permute-start.19 = (bf16[112,4096]{1,0:T(8,128)(2,1)}, bf16[112,4096]{1,0:T(8,128)(2,1)}, u32[]{:S(2)}, u32[]{:S(2)}) collective-permute-start(bf16[112,4096]{1,0:T(8,128)(2,1)} %get-tuple-element.285.refs_0_), channel_id=1, source_target_pairs={{0,1},{1,0},{2,3},{3,2},{4,5},{5,4},{6,7},{7,6},{8,9},{9,8},{10,11... | collective-permute-start | bytes 2752520 | tf_op jit(solution)/shard_map/cond/branch_1_fun/ppermute | solution.py:239
  140.0 39.0 %collective-permute-start.20 = (s16[240,2048]{1,0:T(8,128)(2,1)}, s16[240,2048]{1,0:T(8,128)(2,1)S(1)}, u32[]{:S(2)}, u32[]{:S(2)}) collective-permute-start(s16[240,2048]{1,0:T(8,128)(2,1)} %get-tuple-element.295), channel_id=1, source_target_pairs={{0,8},{24,16},{1,9},{25,17},{2,10},{26,18},{3,11},{27,19},{4,12},{... | collective-permute-start | bytes 2949128 | tf_op jit(solution)/shard_map/cond/branch_1_fun/ppermute | solution.py:248
  141.3 37.7 %collective-permute-start.21 = (s16[240,2048]{1,0:T(8,128)(2,1)}, s16[240,2048]{1,0:T(8,128)(2,1)}, u32[]{:S(2)}, u32[]{:S(2)}) collective-permute-start(s16[240,2048]{1,0:T(8,128)(2,1)} %get-tuple-element.296), channel_id=1, source_target_pairs={{8,24},{16,0},{9,25},{17,1},{10,26},{18,2},{11,27},{19,3},{12,28},... | collective-permute-start | bytes 2949128 | tf_op jit(solution)/shard_map/cond/branch_1_fun/ppermute | solution.py:257
  152.1 37.3 %collective-permute-start.22 = (s16[240,2048]{1,0:T(8,128)(2,1)S(1)}, s16[240,2048]{1,0:T(8,128)(2,1)S(1)}, u32[]{:S(2)}, u32[]{:S(2)}) collective-permute-start(s16[240,2048]{1,0:T(8,128)(2,1)S(1)} %branch_1_fun.25), channel_id=1, source_target_pairs={{8,16},{16,8},{9,17},{17,9},{10,18},{18,10},{11,19},{19,11},{12,20... | collective-permute-start | bytes 2949128 | tf_op jit(solution)/shard_map/cond/branch_1_fun/ppermute | solution.py:251
  165.6 23.8 %collective-permute-start.23 = (s16[240,2048]{1,0:T(8,128)(2,1)S(1)}, s16[240,2048]{1,0:T(8,128)(2,1)S(1)}, u32[]{:S(2)}, u32[]{:S(2)}) collective-permute-start(s16[240,2048]{1,0:T(8,128)(2,1)S(1)} %get-tuple-element.299), channel_id=1, source_target_pairs={{16,24},{8,0},{17,25},{9,1},{18,26},{10,2},{19,27},{11,3},{20,28},... | collective-permute-start | bytes 2949128 | tf_op jit(solution)/shard_map/cond/branch_1_fun/ppermute | solution.py:260
  194.5 25.1 %collective-permute-start.26 = (s16[240,2048]{1,0:T(8,128)(2,1)}, s16[240,2048]{1,0:T(8,128)(2,1)S(1)}, u32[]{:S(2)}, u32[]{:S(2)}) collective-permute-start(s16[240,2048]{1,0:T(8,128)(2,1)} %get-tuple-element.334), channel_id=1, source_target_pairs={{0,16},{24,8},{1,17},{25,9},{2,18},{26,10},{3,19},{27,11},{4,20},{... | collective-permute-start | bytes 2949128 | tf_op jit(solution)/shard_map/cond/branch_1_fun/ppermute | solution.py:254
  195.8 25.0 %collective-permute-start.27 = (s16[240,2048]{1,0:T(8,128)(2,1)}, s16[240,2048]{1,0:T(8,128)(2,1)S(1)}, u32[]{:S(2)}, u32[]{:S(2)}) collective-permute-start(s16[240,2048]{1,0:T(8,128)(2,1)} %get-tuple-element.335), channel_id=1, source_target_pairs={{16,24},{8,0},{17,25},{9,1},{18,26},{10,2},{19,27},{11,3},{20,28},... | collective-permute-start | bytes 2949128 | tf_op jit(solution)/shard_map/cond/branch_1_fun/ppermute | solution.py:260
  200.9 24.4 %collective-permute-start.24 = (s16[128,2048]{1,0:T(8,128)(2,1)S(1)}, s16[128,2048]{1,0:T(8,128)(2,1)}, u32[]{:S(2)}, u32[]{:S(2)}) collective-permute-start(s16[128,2048]{1,0:T(8,128)(2,1)S(1)} %get-tuple-element.302), channel_id=1, source_target_pairs={{0,2},{1,3},{2,0},{3,1},{4,6},{5,7},{6,4},{7,5},{8,10},{9,11},{10,... | collective-permute-start | bytes 1572872 | tf_op jit(solution)/shard_map/cond/branch_1_fun/ppermute | solution.py:239
  201.2 24.7 %collective-permute-start.25 = (s16[128,2048]{1,0:T(8,128)(2,1)}, s16[128,2048]{1,0:T(8,128)(2,1)}, u32[]{:S(2)}, u32[]{:S(2)}) collective-permute-start(s16[128,2048]{1,0:T(8,128)(2,1)} %get-tuple-element.303), channel_id=1, source_target_pairs={{0,3},{1,2},{2,1},{3,0},{4,7},{5,6},{6,5},{7,4},{8,11},{9,10},{10,... | collective-permute-start | bytes 1572872 | tf_op jit(solution)/shard_map/cond/branch_1_fun/ppermute | solution.py:239
  (14 other events, 97.8 us)
